TPU v7x, 128 devices: a whole 4x4x4 slice. The times are simulated.
128 devices in a mesh: dp: 32 (over z, y, core), mp: 4 (over x).
Axes of the slice: x: 4, y: 4, z: 4, core: 2. Of those that a mesh axis runs over, the one named last changes fastest.
Arguments:
- patches: bfloat16 [49152, 128], P(('dp', 'mp')), may hold values from -6 to 6
- row_count: int32 [128], P(('dp', 'mp')), may hold values from 0 to 384, as said below
- target_group: int32 [49152], P(('dp', 'mp')), may hold values from 0 to 31, as said below
- target_offset: int32 [49152], P(('dp', 'mp')), may hold values from 0 to 639, as said below
- embed: bfloat16 [128, 6144], replicated, may hold values from -0.5 to 0.5
- norm_gain: bfloat16 [6144], replicated, may hold values from 0.099609375 to 1.8984375
- readout: bfloat16 [6144, 128], P('mp'), may hold values from -0.078125 to 0.078125
- target: bfloat16 [20480, 128], P('dp'), may hold values from -12 to 12
- master: float32 [6144, 6144], P('dp', 'mp'), may hold values from -6 to 6
- moment1: float32 [6144, 6144], P('dp', 'mp'), may hold values from -2 to 2
- moment2: float32 [6144, 6144], P('dp', 'mp'), may hold values from 0.0034722222 to 0.1388889
Outputs:
- prediction: float32 [20480, 128], P('dp')
- master_new: float32 [6144, 6144], P('dp', 'mp')
- moment1_new: float32 [6144, 6144], P('dp', 'mp')
- moment2_new: float32 [6144, 6144], P('dp', 'mp')
- weight_copy: bfloat16 [6144, 6144], P('dp', 'mp')
Inputs may be any that keep to these rules, and one draw needn't show every extreme that they name: Device i holds its live patch rows in its first row_count[i] slots; some device holds 384 of them in every draw. Over the live slots of all devices, each pair (target_group, target_offset) of the 20480 positions occurs exactly once; values in slots past row_count are arbitrary within the range. Call target_offset // 160 the block of a row. Each (batch, block) receives exactly 160 live rows; one device sends at most 3 live rows to one (batch, block), and every (batch, block) gets 3 rows from some device.
All inputs are finite; a program needn't handle non-finite values.
Results may differ from a plain program's by a relative error of at most 0.03.
Values may be sent and summed in bfloat16 or wider, within the bound.
A program may use at most 128 MiB of HBM per device.

v0:
```python
import jax
import jax.numpy as jnp
from jax import lax
from jax.sharding import PartitionSpec as P

gelu_const = 0.7978845608028654
beta_one = 0.9
beta_two = 0.95
learn_rate = 0.01
decay_rate = 0.1
adam_epsilon = 1e-08
step_count = 20


def gelu_tanh(value):
    inner = gelu_const * (value + 0.044715 * value * value * value)
    return 0.5 * value * (1.0 + jnp.tanh(inner))


def gelu_slope(value):
    tangent = jnp.tanh(gelu_const * (value + 0.044715 * value * value * value))
    return 0.5 * (1.0 + tangent) + 0.5 * value * (1.0 - tangent * tangent) * gelu_const * (
        1.0 + 3.0 * 0.044715 * value * value
    )


def shards(
    patches,
    row_count,
    target_group,
    target_offset,
    embed,
    norm_gain,
    readout,
    target,
    master,
    moment1,
    moment2,
):
    model_count = lax.axis_size("mp")
    batch_count = lax.axis_size("dp")
    devices_all = batch_count * model_count
    slot_total = patches.shape[0]
    capacity = slot_total // devices_all
    batch_rows = target.shape[0]
    block_rows = batch_rows // model_count
    width = embed.shape[1]
    patch_width = patches.shape[1]
    occupied = jnp.arange(slot_total, dtype=jnp.int32) < row_count[0]
    owner_index = jnp.where(
        occupied, target_group * model_count + target_offset // block_rows, devices_all
    )
    onehot = (owner_index[:, None] == jnp.arange(devices_all, dtype=jnp.int32)[None, :]).astype(
        jnp.int32
    )
    running = jnp.cumsum(onehot, axis=0)
    placing = jnp.sum(onehot * running, axis=1) - 1
    send_slot = jnp.where(occupied, owner_index * capacity + placing, devices_all * capacity)
    outgoing = (
        jnp.zeros((devices_all * capacity, patch_width), jnp.bfloat16)
        .at[send_slot]
        .set(patches, mode="drop")
    )
    slot_marks = (
        jnp.full((devices_all * capacity,), block_rows, jnp.int32)
        .at[send_slot]
        .set(target_offset % block_rows, mode="drop")
    )
    arrived, arrived_marks = (
        lax.all_to_all(outgoing, ("dp", "mp"), split_axis=0, concat_axis=0, tiled=True),
        lax.all_to_all(slot_marks, ("dp", "mp"), split_axis=0, concat_axis=0, tiled=True),
    )
    block_patches = (
        jnp.zeros((block_rows, patch_width), jnp.bfloat16)
        .at[arrived_marks]
        .set(arrived, mode="drop")
    )
    gain_wide = norm_gain.astype(jnp.float32)
    hidden = gelu_tanh(
        jnp.dot(
            lax.all_gather(block_patches, "mp", axis=0, tiled=True),
            embed,
            preferred_element_type=jnp.float32,
        )
    )
    normed = (
        hidden * lax.rsqrt(jnp.mean(hidden * hidden, axis=-1, keepdims=True) + 1e-05) * gain_wide
    ).astype(jnp.bfloat16)
    weight = master.astype(jnp.bfloat16)
    width_scale = 1.0 / width**0.5
    columns = normed
    preact = (
        jnp.dot(
            columns,
            lax.all_gather(weight, "dp", axis=0, tiled=True),
            preferred_element_type=jnp.float32,
        )
        * width_scale
    )
    activation = gelu_tanh(preact).astype(jnp.bfloat16)
    prediction = lax.psum(
        jnp.dot(activation, readout, preferred_element_type=jnp.float32).astype(jnp.bfloat16), "mp"
    ).astype(jnp.float32)
    errors = (prediction - target.astype(jnp.float32)).astype(jnp.bfloat16)
    backward = lax.dot_general(
        errors, readout, (((1,), (1,)), ((), ())), preferred_element_type=jnp.float32
    )
    delta_rows = (backward * gelu_slope(preact)).astype(jnp.bfloat16)
    columns = normed
    gradient = lax.psum_scatter(
        (
            lax.dot_general(
                columns, delta_rows, (((0,), (0,)), ((), ())), preferred_element_type=jnp.float32
            )
            * width_scale
        ).astype(jnp.bfloat16),
        "dp",
        scatter_dimension=0,
        tiled=True,
    ).astype(jnp.float32)
    moment1_new = beta_one * moment1 + (1.0 - beta_one) * gradient
    moment2_new = beta_two * moment2 + (1.0 - beta_two) * gradient * gradient
    first_fix = moment1_new / (1.0 - beta_one**step_count)
    second_fix = moment2_new / (1.0 - beta_two**step_count)
    master_new = master - learn_rate * (
        first_fix / (jnp.sqrt(second_fix) + adam_epsilon) + decay_rate * master
    )
    return (prediction, master_new, moment1_new, moment2_new, master_new.astype(jnp.bfloat16))


def solution(mesh):
    placed = (
        P(("dp", "mp"), None),
        P(("dp", "mp")),
        P(("dp", "mp")),
        P(("dp", "mp")),
        P(),
        P(),
        P("mp", None),
        P("dp", None),
        P("dp", "mp"),
        P("dp", "mp"),
        P("dp", "mp"),
    )
    return jax.shard_map(
        shards,
        mesh=mesh,
        in_specs=placed,
        out_specs=(P("dp", None), P("dp", "mp"), P("dp", "mp"), P("dp", "mp"), P("dp", "mp")),
        check_vma=False,
    )
```

profile of v0, /device:TPU:0, one launch (start us, length us, event | category | flops | bytes accessed | tf_op | source)
XLA Modules:
  0.0 316.7 jit_solution(15524870666545750787)
XLA Ops:
  7.2 2.3 convert_element_type.44
  10.2 0.7 add_select_fusion
  10.9 0.1 copy.18
  11.0 0.2 fusion.14
  11.3 0.1 broadcast_add_fusion
  11.3 0.2 fusion.16
  11.6 2.9 scatter_custom_fusion
  14.5 0.8 all_to_all.16
  15.3 11.1 %all-to-all-start = ((s32[128,3,1]{1,2,0:T(1,128)}), s32[128,3,1]{1,2,0:T(1,128)S(1)}, u32[]{:S(2)}, u32[]{:S(2)}) async-start(s32[128,3,1]{1,2,0:T(1,128)} %bitcast.5), calls=%async_computation | async-start | bytes 131072 | tf_op jit(solution)/shard_map/all_to_all | solution.py:71
  26.5 1.8 scatter_custom_fusion.1
  28.3 0.7 all_to_all.19
  29.0 6.7 %all-to-all-done = s32[128,3,1]{1,2,0:T(1,128)S(1)} async-done(((s32[128,3,1]{1,2,0:T(1,128)}), s32[128,3,1]{1,2,0:T(1,128)S(1)}, u32[]{:S(2)}, u32[]{:S(2)}) %all-to-all-start) | async-done | bytes 1568 | tf_op jit(solution)/shard_map/all_to_all | solution.py:71
  35.7 4.6 %all-to-all-start.1 = ((bf16[128,3,128]{2,1,0:T(4,128)(2,1)}), bf16[128,3,128]{2,1,0:T(4,128)(2,1)S(1)}, u32[]{:S(2)}, u32[]{:S(2)}) async-start(bf16[128,3,128]{2,1,0:T(4,128)(2,1)} %all_to_all.19), calls=%async_computation.1 | async-start | bytes 262144 | tf_op jit(solution)/shard_map/all_to_all | solution.py:70
  40.4 0.0 all-reduce.2.cloned.1.call-start
  40.4 0.5 broadcast.113
  40.9 0.8 reduce.5
  41.7 0.2 all_to_all.18
  42.0 7.9 %all-to-all-done.1 = bf16[128,3,128]{2,1,0:T(4,128)(2,1)S(1)} async-done(((bf16[128,3,128]{2,1,0:T(4,128)(2,1)}), bf16[128,3,128]{2,1,0:T(4,128)(2,1)S(1)}, u32[]{:S(2)}, u32[]{:S(2)}) %all-to-all-start.1) | async-done | bytes 98336 | tf_op jit(solution)/shard_map/all_to_all | solution.py:70
  49.8 0.1 reshape.88
  49.9 1.4 scatter_custom_fusion.2
  51.4 12.2 %all_gather.6 = bf16[640,128]{1,0:T(8,128)(2,1)S(1)} all-gather(bf16[160,128]{1,0:T(8,128)(2,1)S(1)} %scatter_custom_fusion.2), channel_id=1, replica_groups=mesh['dp'=32,'mp'=4] {'mp'}, dimensions={0}, use_global_device_ids=true | all-gather | bytes 204800 | tf_op jit(solution)/shard_map/all_gather | solution.py:81
  63.6 9.0 %multiply_reduce_fusion = (f32[640]{0:T(1024)S(1)}, f32[640,6144]{1,0:T(8,128)}) fusion(bf16[640,128]{1,0:T(8,128)(2,1)S(1)} %all_gather.6, bf16[128,6144]{1,0:T(8,128)(2,1)S(1)} %copy-done), kind=kOutput, calls=%fused_computation.10 | convolution fusion | flops 1045953920 | bytes 17467904 | tf_op jit(solution)/shard_map/dot_general | solution.py:80
  72.6 19.0 %all-gather.2.cloned.1.call-done = bf16[6144,1536]{1,0:T(8,128)(2,1)} async-done(((bf16[192,1536]{1,0:T(8,128)(2,1)}), bf16[6144,1536]{1,0:T(8,128)(2,1)}) %all-gather.2.cloned.1.call-update) | async-done | bytes 18874384 | tf_op jit(solution)/shard_map/all_gather | solution.py:95
  91.6 18.6 %fusion.40 = f32[640,1536]{1,0:T(8,128)S(1)} fusion(bf16[6144,1536]{1,0:T(8,128)(2,1)} %all-gather.2.cloned.1.call-done, f32[640,6144]{1,0:T(8,128)} %get-tuple-element.12, f32[6144]{0:T(1024)S(1)} %convert_element_type.42, f32[640]{0:T(1024)S(1)} %add_rsqrt_fusion), kind=kOutput, calls=%fused_computation.67 | convolution fusion | flops 12091392000 | bytes 38562304 | tf_op jit(solution)/shard_map/dot_general | solution.py:93
  110.2 2.0 copy-done.7
  112.2 2.2 fusion.13
  114.4 0.3 reduce-scatter.2.cloned.1.call-start
  114.7 40.5 %all-reduce.2.cloned.1.call-done = bf16[640,128]{1,0:T(8,128)(2,1)} async-done(((bf16[640,128]{1,0:T(8,128)(2,1)}), bf16[640,128]{1,0:T(8,128)(2,1)}) %all-reduce.2.cloned.1.call-update) | async-done | bytes 163856 | tf_op jit(solution)/shard_map/psum | solution.py:101
  155.2 0.9 convert_element_type.47
  156.1 27.2 %multiply_convert_fusion = bf16[6144,1536]{1,0:T(8,128)(2,1)} fusion(f32[640,1536]{1,0:T(8,128)} %copy-done.7, bf16[1536,128]{1,0:T(8,128)(2,1)S(1)} %copy-done.5, f32[640,128]{1,0:T(8,128)S(1)} %convert_element_type.47, bf16[640,128]{1,0:T(8,128)(2,1)S(1)} %copy-done.6, f32[640,6144]{1,0:T(8,128)} %get-tuple-element.12, f32[6144]{0:T(1024)S(1)} %convert_element_type.42, ...), kind=kOutput, calls=%fused_computation.3 | convolution fusion | flops 12381831168 | bytes 39447040 | tf_op jit(solution)/shard_map/dot_general | solution.py:112
  183.4 122.3 %reduce-scatter.2.cloned.1.call-done = bf16[192,1536]{1,0:T(8,128)(2,1)} async-done(((bf16[6144,1536]{1,0:T(8,128)(2,1)}), bf16[192,1536]{1,0:T(8,128)(2,1)}) %reduce-scatter.2.cloned.1.call-update) | async-done | bytes 589840 | tf_op jit(solution)/shard_map/reduce_scatter | solution.py:110
  305.7 4.4 %fusion.41 = (bf16[192,1536]{1,0:T(8,128)(2,1)}, f32[192,1536]{1,0:T(8,128)}, f32[192,1536]{1,0:T(8,128)}, f32[192,1536]{1,0:T(8,128)}) fusion(f32[192,1536]{1,0:T(8,128)S(1)} %copy-done.2, bf16[192,1536]{1,0:T(8,128)(2,1)} %reduce-scatter.2.cloned.1.call-done, f32[192,1536]{1,0:T(8,128)} %param.20, f32[192,1536]{1,0:T(8,128)} %param.21), kind=kLoop, calls=%fused_computation.68 | loop fusion | flops 5013504 | bytes 8257536 | tf_op jit(solution)/shard_map/convert_element_type | solution.py:128
  (26 shorter events, 0.2 us)
Async XLA Ops:
  7.2 56.4 %copy-start = (bf16[128,6144]{1,0:T(8,128)(2,1)S(1)}, bf16[128,6144]{1,0:T(8,128)(2,1)}, u32[]{:S(2)}) copy-start(bf16[128,6144]{1,0:T(8,128)(2,1)} %param.15) | copy-start | bytes 4718596
  7.2 19.3 %copy-start.4 = (bf16[6144]{0:T(1024)(128)(2,1)S(1)}, bf16[6144]{0:T(1024)(128)(2,1)}, u32[]{:S(2)}) copy-start(bf16[6144]{0:T(1024)(128)(2,1)} %param.16) | copy-start | bytes 36868
  7.2 84.4 %all-gather.2.cloned.1.call-start = ((), (), s32[]{:S(2)}) async-start(), calls=%async_computation.3 | async-start | bytes 19464192 | tf_op jit(solution)/shard_map/all_gather | solution.py:95
  15.3 20.4 %all-to-all-start = ((s32[128,3,1]{1,2,0:T(1,128)}), s32[128,3,1]{1,2,0:T(1,128)S(1)}, u32[]{:S(2)}, u32[]{:S(2)}) async-start(s32[128,3,1]{1,2,0:T(1,128)} %bitcast.5), calls=%async_computation | async-start | bytes 131072 | tf_op jit(solution)/shard_map/all_to_all | solution.py:71
  35.7 14.1 %all-to-all-start.1 = ((bf16[128,3,128]{2,1,0:T(4,128)(2,1)}), bf16[128,3,128]{2,1,0:T(4,128)(2,1)S(1)}, u32[]{:S(2)}, u32[]{:S(2)}) async-start(bf16[128,3,128]{2,1,0:T(4,128)(2,1)} %all_to_all.19), calls=%async_computation.1 | async-start | bytes 262144 | tf_op jit(solution)/shard_map/all_to_all | solution.py:70
  40.4 114.8 %all-reduce.2.cloned.1.call-start = ((), (), s32[]{:S(2)}) async-start(), calls=%async_computation.4 | async-start | bytes 327680 | tf_op jit(solution)/shard_map/psum | solution.py:101
  91.6 20.6 %copy-start.5 = (bf16[1536,128]{1,0:T(8,128)(2,1)S(1)}, bf16[1536,128]{1,0:T(8,128)(2,1)}, u32[]{:S(2)}) copy-start(bf16[1536,128]{1,0:T(8,128)(2,1)} %param.17) | copy-start | bytes 1179652
  110.2 2.0 copy-start.7
  112.2 43.9 %copy-start.6 = (bf16[640,128]{1,0:T(8,128)(2,1)S(1)}, bf16[640,128]{1,0:T(8,128)(2,1)}, u32[]{:S(2)}) copy-start(bf16[640,128]{1,0:T(8,128)(2,1)} %param.18) | copy-start | bytes 491524
  114.4 191.3 %reduce-scatter.2.cloned.1.call-start = ((), (), s32[]{:S(2)}) async-start(), calls=%async_computation.5 | async-start | bytes 19464192 | tf_op jit(solution)/shard_map/reduce_scatter | solution.py:110
  156.1 27.3 %copy-start.3 = (f32[640,128]{1,0:T(8,128)}, f32[640,128]{1,0:T(8,128)S(1)}, u32[]{:S(2)}) copy-start(f32[640,128]{1,0:T(8,128)S(1)} %convert_element_type.47) | copy-start | bytes 983044
  183.4 122.3 %copy-start.2 = (f32[192,1536]{1,0:T(8,128)S(1)}, f32[192,1536]{1,0:T(8,128)}, u32[]{:S(2)}) copy-start(f32[192,1536]{1,0:T(8,128)} %param.19) | copy-start | bytes 3538948
  183.4 126.7 %copy-start.1 = (bf16[128,6144]{1,0:T(8,128)(2,1)S(1)}, bf16[128,6144]{1,0:T(8,128)(2,1)}, u32[]{:S(2)}) copy-start(bf16[128,6144]{1,0:T(8,128)(2,1)} %param.15) | copy-start | bytes 4718596
Sparse Core Ops, SparseCore 0:
  10.9 80.6 all-gather.1
  114.5 40.6 all-reduce.1
  183.5 122.1 reduce-scatter.1
where the time goes:
time: 317 us
  waiting for transfers between devices  196 us (62%)
  matrix products  57 us (18%)
  starting transfers between devices  16.1 us (5%)
  between operations  14.6 us (5%)
  blocking collectives  12.2 us (4%)
  local copies, waits for them, and re-layouts  10.7 us (3%)
  other arithmetic  9.67 us (3%)
    reduce_scatter x1, waiting for transfers between devices, shards(): lax.psum_scatter((lax.dot_general(columns, delta_rows, (((0,), (0,)), (()...  122 us
    psum x1, waiting for transfers between devices, shards(): lax.psum(jnp.dot(activation, readout, preferred_element_type=jnp.float32)...  40.5 us
    dot_general x1, matrix products, shards(): lax.dot_general(columns, delta_rows, (((0,), (0,)), ((), ())), preferred_...  27.2 us
    all_gather x1, waiting for transfers between devices, shards(): lax.all_gather(weight, 'dp', axis=0, tiled=True)  19 us
    dot_general x1, matrix products, shards(): jnp.dot(columns, lax.all_gather(weight, 'dp', axis=0, tiled=True), prefer...  18.6 us
    all_gather x1, blocking collectives, shards(): lax.all_gather(block_patches, 'mp', axis=0, tiled=True)  12.2 us
    all_to_all x1, starting transfers between devices, shards(): lax.all_to_all(slot_marks, ('dp', 'mp'), split_axis=0, concat_axis=0, til...  11.1 us
    dot_general x1, matrix products, shards(): jnp.dot(lax.all_gather(block_patches, 'mp', axis=0, tiled=True), embed, p...  8.99 us
  transfers between devices with their start and end apart: 5, of which 5 were waited for; matrix products, arithmetic and copies ran while one was open for 6% of the time, Pallas kernels for 0%

commit v1 on v0

--- a/solution.py
+++ b/solution.py
@@ -10,6 +10,12 @@
 decay_rate = 0.1
 adam_epsilon = 1e-08
 step_count = 20
+
+
+def summed_here(x, name):
+    parts = lax.all_gather(x, name, axis=0, tiled=False)
+    result = parts.sum(axis=0)
+    return result
 
 
 def gelu_tanh(value):
@@ -98,7 +104,7 @@
         * width_scale
     )
     activation = gelu_tanh(preact).astype(jnp.bfloat16)
-    prediction = lax.psum(
+    prediction = summed_here(
         jnp.dot(activation, readout, preferred_element_type=jnp.float32).astype(jnp.bfloat16), "mp"
     ).astype(jnp.float32)
     errors = (prediction - target.astype(jnp.float32)).astype(jnp.bfloat16)

time: 317 us -> 286 us (0.902)
  waiting for transfers between devices: 196 us -> 155 us
  blocking collectives: 12.2 us -> 26 us
    psum x1 -> x0, waiting for transfers between devices: 40.5 us -> none  [shards(): lax.psum(jnp.dot(activation, readout, preferred_element_type=jnp.float32)...]
    all_gather x0 -> x1, blocking collectives: none -> 13.7 us  [summed_here(): parts = lax.all_gather(x, name, axis=0, tiled=False)]
  transfers between devices with their start and end apart: 5 -> 4, of which waited for: 5 -> 4; matrix products, arithmetic and copies ran while one was open for 6% -> 6% of each run, Pallas kernels for 0% -> 0%
where the time goes in v1:
time: 286 us
  waiting for transfers between devices  155 us (54%)
  matrix products  56.4 us (20%)
  blocking collectives  26 us (9%)
  starting transfers between devices  15.9 us (6%)
  between operations  14.9 us (5%)
  local copies, waits for them, and re-layouts  9.17 us (3%)
  other arithmetic  8.88 us (3%)
    reduce_scatter x1, waiting for transfers between devices, shards(): lax.psum_scatter((lax.dot_general(columns, delta_rows, (((0,), (0,)), (()...  121 us
    dot_general x1, matrix products, shards(): lax.dot_general(columns, delta_rows, (((0,), (0,)), ((), ())), preferred_...  27.3 us
    all_gather x1, waiting for transfers between devices, shards(): lax.all_gather(weight, 'dp', axis=0, tiled=True)  19 us
    dot_general x1, matrix products, shards(): jnp.dot(columns, lax.all_gather(weight, 'dp', axis=0, tiled=True), prefer...  18.6 us
    all_gather x1, blocking collectives, summed_here(): parts = lax.all_gather(x, name, axis=0, tiled=False)  13.7 us
    all_gather x1, blocking collectives, shards(): lax.all_gather(block_patches, 'mp', axis=0, tiled=True)  12.2 us
    all_to_all x1, starting transfers between devices, shards(): lax.all_to_all(slot_marks, ('dp', 'mp'), split_axis=0, concat_axis=0, til...  11.1 us
    dot_general x1, matrix products, shards(): jnp.dot(lax.all_gather(block_patches, 'mp', axis=0, tiled=True), embed, p...  8.99 us
  transfers between devices with their start and end apart: 4, of which 4 were waited for; matrix products, arithmetic and copies ran while one was open for 6% of the time, Pallas kernels for 0%

profile of v1, /device:TPU:0, one launch (start us, length us, event | category | flops | bytes accessed | tf_op | source)
XLA Modules:
  0.0 286.1 jit_solution(13497228313792468630)
XLA Ops:
  7.2 0.0 all-gather.3.cloned.1.call-start
  7.2 2.3 convert_element_type.46
  10.2 0.7 add_select_fusion
  10.9 0.1 copy.18
  11.0 0.2 fusion.14
  11.3 0.1 broadcast_add_fusion
  11.3 0.2 fusion.16
  11.6 2.9 %scatter_custom_fusion = s32[384]{0:T(512)S(1)} fusion(s32[384]{0:T(512)S(1)} %compare_select_fusion.1, s32[384]{0:T(512)S(1)} %get-tuple-element.9, s32[]{:T(128)} %constant.29.clone.1), kind=kCustom, calls=%fused_computation.53 | custom fusion | bytes 1540 | tf_op jit(solution)/shard_map/scatter | solution.py:73
  14.5 0.8 all_to_all.16
  15.3 11.1 %all-to-all-start = ((s32[128,3,1]{1,2,0:T(1,128)}), s32[128,3,1]{1,2,0:T(1,128)S(1)}, u32[]{:S(2)}, u32[]{:S(2)}) async-start(s32[128,3,1]{1,2,0:T(1,128)} %bitcast.5), calls=%async_computation | async-start | bytes 131072 | tf_op jit(solution)/shard_map/all_to_all | solution.py:77
  26.5 1.8 scatter_custom_fusion.1
  28.3 0.7 all_to_all.19
  29.0 6.7 %all-to-all-done = s32[128,3,1]{1,2,0:T(1,128)S(1)} async-done(((s32[128,3,1]{1,2,0:T(1,128)}), s32[128,3,1]{1,2,0:T(1,128)S(1)}, u32[]{:S(2)}, u32[]{:S(2)}) %all-to-all-start) | async-done | bytes 1568 | tf_op jit(solution)/shard_map/all_to_all | solution.py:77
  35.7 4.6 %all-to-all-start.1 = ((bf16[128,3,128]{2,1,0:T(4,128)(2,1)}), bf16[128,3,128]{2,1,0:T(4,128)(2,1)S(1)}, u32[]{:S(2)}, u32[]{:S(2)}) async-start(bf16[128,3,128]{2,1,0:T(4,128)(2,1)} %all_to_all.19), calls=%async_computation.1 | async-start | bytes 262144 | tf_op jit(solution)/shard_map/all_to_all | solution.py:76
  40.4 0.0 reduce-scatter.2.cloned.1.call-start
  40.4 0.5 broadcast.113
  40.9 0.8 reduce.6
  41.7 0.2 all_to_all.18
  42.0 7.9 %all-to-all-done.1 = bf16[128,3,128]{2,1,0:T(4,128)(2,1)S(1)} async-done(((bf16[128,3,128]{2,1,0:T(4,128)(2,1)}), bf16[128,3,128]{2,1,0:T(4,128)(2,1)S(1)}, u32[]{:S(2)}, u32[]{:S(2)}) %all-to-all-start.1) | async-done | bytes 98336 | tf_op jit(solution)/shard_map/all_to_all | solution.py:76
  49.8 0.1 reshape.88
  49.9 1.4 scatter_custom_fusion.2
  51.4 12.2 %all_gather.12 = bf16[640,128]{1,0:T(8,128)(2,1)S(1)} all-gather(bf16[160,128]{1,0:T(8,128)(2,1)S(1)} %scatter_custom_fusion.2), channel_id=1, replica_groups=mesh['dp'=32,'mp'=4] {'mp'}, dimensions={0}, use_global_device_ids=true | all-gather | bytes 204800 | tf_op jit(solution)/shard_map/all_gather | solution.py:87
  63.6 9.0 %multiply_reduce_fusion = (f32[640]{0:T(1024)S(1)}, f32[640,6144]{1,0:T(8,128)}) fusion(bf16[640,128]{1,0:T(8,128)(2,1)S(1)} %all_gather.12, bf16[128,6144]{1,0:T(8,128)(2,1)S(1)} %copy-done), kind=kOutput, calls=%fused_computation.10 | convolution fusion | flops 1045953920 | bytes 17467904 | tf_op jit(solution)/shard_map/dot_general | solution.py:86
  72.6 19.0 %all-gather.3.cloned.1.call-done = bf16[6144,1536]{1,0:T(8,128)(2,1)} async-done(((bf16[192,1536]{1,0:T(8,128)(2,1)}), bf16[6144,1536]{1,0:T(8,128)(2,1)}) %all-gather.3.cloned.1.call-update) | async-done | bytes 18874384 | tf_op jit(solution)/shard_map/all_gather | solution.py:101
  91.6 18.6 %fusion.40 = f32[640,1536]{1,0:T(8,128)S(1)} fusion(bf16[6144,1536]{1,0:T(8,128)(2,1)} %all-gather.3.cloned.1.call-done, f32[640,6144]{1,0:T(8,128)} %get-tuple-element.12, f32[6144]{0:T(1024)S(1)} %convert_element_type.44, f32[640]{0:T(1024)S(1)} %add_rsqrt_fusion), kind=kOutput, calls=%fused_computation.67 | convolution fusion | flops 12091392000 | bytes 38562304 | tf_op jit(solution)/shard_map/dot_general | solution.py:99
  110.2 1.5 fusion.13
  111.7 0.5 copy-done.7
  112.2 13.7 %all-gather = bf16[2560,128]{1,0:T(8,128)(2,1)S(1)} all-gather(bf16[640,128]{1,0:T(8,128)(2,1)S(1)} %fusion.13), channel_id=2, replica_groups=mesh['dp'=32,'mp'=4] {'mp'}, dimensions={0}, use_global_device_ids=true | all-gather | bytes 819200 | tf_op jit(solution)/shard_map/all_gather | solution.py:16
  125.9 0.1 reduce_sum.32
  126.1 27.3 %multiply_convert_fusion = bf16[6144,1536]{1,0:T(8,128)(2,1)} fusion(f32[640,1536]{1,0:T(8,128)} %copy-done.7, bf16[1536,128]{1,0:T(8,128)(2,1)S(1)} %copy-done.5, f32[640,128]{1,0:T(8,128)S(1)} %convert_element_type.49, bf16[640,128]{1,0:T(8,128)(2,1)S(1)} %copy-done.6, f32[640,6144]{1,0:T(8,128)} %get-tuple-element.12, f32[6144]{0:T(1024)S(1)} %convert_element_type.44, ...), kind=kOutput, calls=%fused_computation.3 | convolution fusion | flops 12381831168 | bytes 39447040 | tf_op jit(solution)/shard_map/dot_general | solution.py:118
  153.4 121.5 %reduce-scatter.2.cloned.1.call-done = bf16[192,1536]{1,0:T(8,128)(2,1)} async-done(((bf16[6144,1536]{1,0:T(8,128)(2,1)}), bf16[192,1536]{1,0:T(8,128)(2,1)}) %reduce-scatter.2.cloned.1.call-update) | async-done | bytes 589840 | tf_op jit(solution)/shard_map/reduce_scatter | solution.py:116
  274.9 4.4 %fusion.41 = (bf16[192,1536]{1,0:T(8,128)(2,1)}, f32[192,1536]{1,0:T(8,128)}, f32[192,1536]{1,0:T(8,128)}, f32[192,1536]{1,0:T(8,128)}) fusion(f32[192,1536]{1,0:T(8,128)S(1)} %copy-done.2, bf16[192,1536]{1,0:T(8,128)(2,1)} %reduce-scatter.2.cloned.1.call-done, f32[192,1536]{1,0:T(8,128)} %param.20, f32[192,1536]{1,0:T(8,128)} %param.21), kind=kLoop, calls=%fused_computation.68 | loop fusion | flops 5013504 | bytes 8257536 | tf_op jit(solution)/shard_map/convert_element_type | solution.py:134
  (25 shorter events, 0.2 us)
Async XLA Ops:
  7.2 56.4 %copy-start = (bf16[128,6144]{1,0:T(8,128)(2,1)S(1)}, bf16[128,6144]{1,0:T(8,128)(2,1)}, u32[]{:S(2)}) copy-start(bf16[128,6144]{1,0:T(8,128)(2,1)} %param.15) | copy-start | bytes 4718596
  7.2 19.3 %copy-start.4 = (bf16[6144]{0:T(1024)(128)(2,1)S(1)}, bf16[6144]{0:T(1024)(128)(2,1)}, u32[]{:S(2)}) copy-start(bf16[6144]{0:T(1024)(128)(2,1)} %param.16) | copy-start | bytes 36868
  7.2 84.4 %all-gather.3.cloned.1.call-start = ((), (), s32[]{:S(2)}) async-start(), calls=%async_computation.3 | async-start | bytes 19464192 | tf_op jit(solution)/shard_map/all_gather | solution.py:101
  15.3 20.4 %all-to-all-start = ((s32[128,3,1]{1,2,0:T(1,128)}), s32[128,3,1]{1,2,0:T(1,128)S(1)}, u32[]{:S(2)}, u32[]{:S(2)}) async-start(s32[128,3,1]{1,2,0:T(1,128)} %bitcast.5), calls=%async_computation | async-start | bytes 131072 | tf_op jit(solution)/shard_map/all_to_all | solution.py:77
  35.7 14.1 %all-to-all-start.1 = ((bf16[128,3,128]{2,1,0:T(4,128)(2,1)}), bf16[128,3,128]{2,1,0:T(4,128)(2,1)S(1)}, u32[]{:S(2)}, u32[]{:S(2)}) async-start(bf16[128,3,128]{2,1,0:T(4,128)(2,1)} %all_to_all.19), calls=%async_computation.1 | async-start | bytes 262144 | tf_op jit(solution)/shard_map/all_to_all | solution.py:76
  40.4 234.5 %reduce-scatter.2.cloned.1.call-start = ((), (), s32[]{:S(2)}) async-start(), calls=%async_computation.4 | async-start | bytes 19464192 | tf_op jit(solution)/shard_map/reduce_scatter | solution.py:116
  91.6 18.6 %copy-start.5 = (bf16[1536,128]{1,0:T(8,128)(2,1)S(1)}, bf16[1536,128]{1,0:T(8,128)(2,1)}, u32[]{:S(2)}) copy-start(bf16[1536,128]{1,0:T(8,128)(2,1)} %param.17) | copy-start | bytes 1179652
  110.2 2.0 copy-start.7
  110.2 15.9 %copy-start.6 = (bf16[640,128]{1,0:T(8,128)(2,1)S(1)}, bf16[640,128]{1,0:T(8,128)(2,1)}, u32[]{:S(2)}) copy-start(bf16[640,128]{1,0:T(8,128)(2,1)} %param.18) | copy-start | bytes 491524
  126.1 27.3 %copy-start.3 = (f32[640,128]{1,0:T(8,128)}, f32[640,128]{1,0:T(8,128)S(1)}, u32[]{:S(2)}) copy-start(f32[640,128]{1,0:T(8,128)S(1)} %convert_element_type.49) | copy-start | bytes 983044
  153.4 121.5 %copy-start.2 = (f32[192,1536]{1,0:T(8,128)S(1)}, f32[192,1536]{1,0:T(8,128)}, u32[]{:S(2)}) copy-start(f32[192,1536]{1,0:T(8,128)} %param.19) | copy-start | bytes 3538948
  153.4 125.9 %copy-start.1 = (bf16[128,6144]{1,0:T(8,128)(2,1)S(1)}, bf16[128,6144]{1,0:T(8,128)(2,1)}, u32[]{:S(2)}) copy-start(bf16[128,6144]{1,0:T(8,128)(2,1)} %param.15) | copy-start | bytes 4718596
Sparse Core Ops, SparseCore 0:
  10.9 80.6 all-gather.2
  153.5 121.3 reduce-scatter.1
